TPU v7x, 32 devices: a whole 2x2x4 slice. The times are simulated.
32 devices in a mesh: section: 4 (over y, core), seq: 8 (over z, x).
Axes of the slice: x: 2, y: 2, z: 4, core: 2. Of those that a mesh axis runs over, the one named last changes fastest.
Arguments:
- activations: bfloat16 [4, 4096, 2048], P('section', 'seq'), may hold values from -6 to 6
- norm_gain: float32 [4, 2048], P('section'), may hold values from 0.5 to 1.5
- value_weight: bfloat16 [4, 2048, 1024], P('section'), may hold values from -0.125 to 0.125
- shared_weight: bfloat16 [4, 2048, 256], P('section'), may hold values from -0.125 to 0.125
- rate_weight: bfloat16 [4, 2048, 8], P('section'), may hold values from -0.125 to 0.125
- rate_bias: float32 [4, 8], P('section'), may hold values from -1 to 1
- decay_rate: float32 [4, 8], P('section'), may hold values from 0.00012207031 to 0.03
- level_table: float32 [4, 16, 13, 8], P('section'), may hold values from 0.25 to 2
- level_ids: int32 [4, 4096, 13], P('section', 'seq'), may hold values from 0 to 15
- out_gain: float32 [4, 1024], P('section'), may hold values from 0.5 to 1.5
- out_weight: bfloat16 [4, 1024, 2048], P('section'), may hold values from -0.1875 to 0.1875
Outputs:
- result: bfloat16 [4, 4096, 2048], P('section', 'seq')
All inputs are finite; a program needn't handle non-finite values.
Results may differ from a plain program's by a relative error of at most 0.03.
Values may be sent and summed in bfloat16 or wider, within the bound.
A program may use at most 128 MiB of HBM per device.

v0:
```python
import functools

import jax
import jax.numpy as jnp
from jax import lax
from jax.experimental import pallas as pl
from jax.experimental.pallas import tpu as pltpu
from jax.sharding import PartitionSpec as P

EPSILON = 1e-05
CHUNK = 128
SLOT = 16
F32 = jnp.float32
BF16 = jnp.bfloat16


def dot(a, b):
    return jnp.dot(a, b, preferred_element_type=F32)


def dot_nt(a, b):
    return lax.dot_general(a, b, (((1,), (1,)), ((), ())), preferred_element_type=F32)


def dot_tn(a, b):
    return lax.dot_general(a, b, (((0,), (0,)), ((), ())), preferred_element_type=F32)


def iota(shape, dim):
    return lax.broadcasted_iota(jnp.int32, shape, dim)


def split3(x):
    hi = x.astype(BF16)
    rest = x - hi.astype(F32)
    mid = rest.astype(BF16)
    return hi, mid, (rest - mid.astype(F32)).astype(BF16)


def spread(row, heads, width):
    rows = row.shape[0]
    return jnp.concatenate(
        [
            jnp.broadcast_to(row[:, h * SLOT : h * SLOT + 1], (rows, width))
            for h in range(heads)
        ],
        axis=1,
    )


def weights_kernel(ids_ref, table_ref, lw_ref):
    lanes = table_ref.shape[0]
    pick = (iota((ids_ref.shape[1], lanes), 0) == iota((ids_ref.shape[1], lanes), 1) // SLOT)
    ids = dot(ids_ref[...], pick.astype(BF16))
    onehot = (ids == (iota(ids.shape, 1) % SLOT).astype(F32)).astype(BF16)
    hi, mid, lo = split3(table_ref[...])
    lw_ref[...] = dot(onehot, hi) + dot(onehot, mid) + dot(onehot, lo)


def tick_kernel(
    heads,
    bits,
    tok_bits,
    x_ref,
    gain_ref,
    wv_ref,
    ws_ref,
    wr_ref,
    bias_ref,
    rate_ref,
    lw_ref,
    out_gain_ref,
    wo_ref,
    y_ref,
    normed,
    step,
    local,
    vals,
    qk,
    acc,
    nmix,
    parts,
    inner,
    subtree,
    send,
    recv,
    send_sem,
    recv_sem,
):
    rows, width = x_ref.shape
    inner_width = heads * CHUNK
    n = CHUNK
    chunks = rows // CHUNK
    inner_bits = chunks.bit_length() - 1
    base = tok_bits - inner_bits
    me = lax.axis_index("seq")

    def bit_of(d):
        return (me // (1 << d)) % 2

    def partner_of(d):
        return me + (1 << d) * (1 - 2 * bit_of(d))

    barrier = pltpu.get_barrier_semaphore()
    for d in range(bits):
        pl.semaphore_signal(barrier, inc=1, device_id={"seq": partner_of(d)}, device_id_type=pl.DeviceIdType.MESH)
    pl.semaphore_wait(barrier, bits)

    @pl.loop(0, chunks)
    def _(c):
        at = pl.ds(pl.multiple_of(c * CHUNK, CHUNK), CHUNK)
        x = x_ref[at, :].astype(F32)
        scale = lax.rsqrt(jnp.mean(x * x, axis=-1, keepdims=True) + EPSILON)
        normed[at, :] = (x * scale * gain_ref[...]).astype(BF16)

    u = dot(normed[...], wr_ref[...]) + bias_ref[...]
    step[...] = jnp.maximum(u, 0.0) + jnp.log1p(jnp.exp(-jnp.abs(u)))
    tri = (iota((CHUNK, CHUNK), 0) >= iota((CHUNK, CHUNK), 1)).astype(BF16)

    totals = []
    for c in range(chunks):
        at = slice(c * CHUNK, (c + 1) * CHUNK)
        hi, mid, lo = split3(-rate_ref[...] * step[at, :])
        cs = dot(tri, hi) + dot(tri, mid) + dot(tri, lo)
        local[at, :] = cs
        totals.append(cs[CHUNK - 1 :, :])

    qk[...] = dot(normed[...], ws_ref[...]).astype(BF16)
    pair = 2 * CHUNK
    for c in range(inner_width // pair):
        raw = dot(normed[...], wv_ref[:, c * pair : (c + 1) * pair])
        for h in (2 * c, 2 * c + 1):
            col = slice((h - 2 * c) * CHUNK, (h - 2 * c + 1) * CHUNK)
            vals[:, h * CHUNK : (h + 1) * CHUNK] = (
                raw[:, col] * step[:, h * SLOT : h * SLOT + 1]
            ).astype(BF16)

    for c in range(chunks):
        at = slice(c * CHUNK, (c + 1) * CHUNK)
        fade = jnp.exp(totals[c] - local[at, :])
        decayed = (vals[at, :].astype(F32) * spread(fade, heads, CHUNK)).astype(BF16)
        parts[at, :] = dot_tn(qk[at, :n], decayed)

    group = {c: (parts[c * CHUNK : (c + 1) * CHUNK, :], totals[c]) for c in range(chunks)}
    slots = []
    for e in range(inner_bits):
        merged = {}
        for g in range(0, len(group), 2):
            (low, low_total), (high, high_total) = group[g], group[g + 1]
            inner[len(slots) * n : (len(slots) + 1) * n, :] = low.astype(BF16)
            slots.append((e, g + 1))
            merged[g // 2] = (
                low * jnp.exp(spread(high_total, heads, CHUNK)) + high,
                low_total + high_total,
            )
        group = merged
    own, total = group[0]
    subtree[...] = own
    total = spread(total, heads, CHUNK)

    def put(d, decay):
        send[d, :n, :] = subtree[...].astype(BF16)
        hi, mid, lo = split3(decay)
        row = iota((SLOT, inner_width), 0)
        tail = jnp.where(row == 0, hi.astype(F32), jnp.where(row == 1, mid.astype(F32), jnp.where(row == 2, lo.astype(F32), 0.0)))
        send[d, n:, :] = tail.astype(BF16)
        copy = pltpu.make_async_remote_copy(
            src_ref=send.at[d],
            dst_ref=recv.at[d],
            send_sem=send_sem.at[d],
            recv_sem=recv_sem.at[d],
            device_id={"seq": partner_of(d)},
            device_id_type=pl.DeviceIdType.MESH,
        )
        copy.start()
        return copy

    position_t = iota((CHUNK, CHUNK), 0)
    position_u = iota((CHUNK, CHUNK), 1)
    causal = position_t >= position_u
    flipped = position_t ^ position_u
    level = jnp.zeros((CHUNK, CHUNK), jnp.int32)
    for b in range(base):
        level = level + (flipped >= (1 << b)).astype(jnp.int32)

    def near(c):
        at = slice(c * CHUNK, (c + 1) * CHUNK)
        scores = jnp.where(causal, dot_nt(qk[at, n:], qk[at, :n]), 0.0)
        run = local[at, :]
        run_t = run.T
        weights = lw_ref[at, :]
        for h in range(heads):
            lane = h * SLOT
            exponent = run[:, lane : lane + 1] - run_t[lane : lane + 1, :]
            weight = jnp.take_along_axis(weights, level + lane, axis=1)
            mixing = (weight * jnp.exp(jnp.minimum(exponent, 0.0)) * scores).astype(BF16)
            col = slice(h * CHUNK, (h + 1) * CHUNK)
            acc[at, col] = dot(mixing, vals[at, col])

    def near_states(c):
        at = slice(c * CHUNK, (c + 1) * CHUNK)
        for slot, (e, g) in enumerate(slots):
            if c >> e != g:
                continue
            prefix = sum([totals[m] for m in range(g << e, c)], jnp.zeros_like(totals[0]))
            coef = lw_ref[at, :] * jnp.exp(local[at, :] + prefix)
            add_level(at, coef, base + e + 1, inner[slot * n : (slot + 1) * n, :])

    def add_level(at, coef, l, state):
        far = dot(qk[at, n:], state)
        for h in range(heads):
            col = slice(h * CHUNK, (h + 1) * CHUNK)
            acc[at, col] += coef[:, h * SLOT + l : h * SLOT + l + 1] * far[:, col]

    def distant(d, prefix):
        upper = bit_of(d) == 1
        factor = jnp.where(upper, jnp.exp(prefix), 0.0)
        state = (recv[d, :n, :].astype(F32) * factor).astype(BF16)
        for c in range(chunks):
            at = slice(c * CHUNK, (c + 1) * CHUNK)
            before = sum(totals[:c], jnp.zeros_like(totals[0]))
            coef = lw_ref[at, :] * jnp.exp(local[at, :] + before)
            add_level(at, coef, tok_bits + 1 + d, state)

    decay = total
    prefix = jnp.zeros_like(total)
    prefixes = []
    work = [functools.partial(near, c) for c in range(chunks)]
    share = -(-len(work) // 2)
    copy = put(0, decay)
    for d in range(bits):
        if d < 2:
            for item in work[d * share : (d + 1) * share]:
                item()
        if d == 1 or bits == 1:
            pass
        if d == 2 or bits < 3 and d == bits - 1:
            for c in range(chunks):
                near_states(c)
        if d >= 2:
            distant(d - 2, prefixes[d - 2])
        copy.wait()
        tail = recv[d, n:, :].astype(F32)
        partner_decay = tail[0:1, :] + tail[1:2, :] + tail[2:3, :]
        prefixes.append(prefix)
        upper = bit_of(d) == 1
        if d < bits - 1:
            mine = jnp.exp(jnp.where(upper, 0.0, partner_decay))
            theirs = jnp.exp(jnp.where(upper, decay, 0.0))
            subtree[...] = subtree[...] * mine + recv[d, :n, :].astype(F32) * theirs
            prefix = jnp.where(upper, prefix + partner_decay, prefix)
            decay = decay + partner_decay
            copy = put(d + 1, decay)
    for d in range(max(bits - 2, 0), bits):
        distant(d, prefixes[d])

    for c in range(chunks):
        at = slice(c * CHUNK, (c + 1) * CHUNK)
        mixed = acc[at, :]
        scale = lax.rsqrt(jnp.mean(mixed * mixed, axis=-1, keepdims=True) + EPSILON)
        nmix[at, :] = (mixed * scale * out_gain_ref[...]).astype(BF16)

    @pl.loop(0, width // pair)
    def _(c):
        at = pl.ds(pl.multiple_of(c * pair, pair), pair)
        y_ref[:, at] = (x_ref[:, at].astype(F32) + dot(nmix[...], wo_ref[:, at])).astype(BF16)


def passed_along(block, axis, distance):
    devices = range(lax.axis_size(axis))
    route = [((i - distance) % len(devices), i) for i in devices]
    return lax.ppermute(block, axis, route)


def vmem(count):
    return [pl.BlockSpec(memory_space=pltpu.VMEM)] * count


def body(
    activations,
    norm_gain,
    value_weight,
    shared_weight,
    rate_weight,
    rate_bias,
    decay_rate,
    level_table,
    level_ids,
    out_gain,
    out_weight,
):
    rows, width = activations.shape[1:]
    heads = rate_bias.shape[1]
    buckets, levels = level_table.shape[1:3]
    inner_width = value_weight.shape[2]
    tok_bits = rows.bit_length() - 1
    bits = lax.axis_size("seq").bit_length() - 1
    chunks = rows // CHUNK
    table = jnp.transpose(level_table[0], (1, 0, 2))
    table = jnp.pad(table, ((0, SLOT - levels), (0, SLOT - buckets), (0, 0)))
    spot = jnp.arange(SLOT)
    table = jnp.where(
        spot[:, None, None, None] == spot[None, None, None, :], table[:, :, :, None], 0.0
    ).reshape(SLOT * SLOT, heads * SLOT)
    ids = jnp.pad(level_ids[0].astype(BF16), ((0, 0), (0, CHUNK - levels)))
    lw = pl.pallas_call(
        weights_kernel,
        out_shape=jax.ShapeDtypeStruct((rows, heads * SLOT), F32),
        in_specs=vmem(2),
        out_specs=vmem(1)[0],
    )(ids, table)
    tick = pl.pallas_call(
        functools.partial(tick_kernel, heads, bits, tok_bits),
        out_shape=jax.ShapeDtypeStruct((rows, width), BF16),
        in_specs=vmem(10),
        out_specs=vmem(1)[0],
        scratch_shapes=[
            pltpu.VMEM((rows, width), BF16),
            pltpu.VMEM((rows, heads * SLOT), F32),
            pltpu.VMEM((rows, heads * SLOT), F32),
            pltpu.VMEM((rows, inner_width), BF16),
            pltpu.VMEM((rows, shared_weight.shape[2]), BF16),
            pltpu.VMEM((rows, inner_width), F32),
            pltpu.VMEM((rows, inner_width), BF16),
            pltpu.VMEM((rows, inner_width), F32),
            pltpu.VMEM((max(chunks - 1, 1) * CHUNK, inner_width), BF16),
            pltpu.VMEM((CHUNK, inner_width), F32),
            pltpu.VMEM((bits, CHUNK + SLOT, inner_width), BF16),
            pltpu.VMEM((bits, CHUNK + SLOT, inner_width), BF16),
            pltpu.SemaphoreType.DMA((bits,)),
            pltpu.SemaphoreType.DMA((bits,)),
        ],
        compiler_params=pltpu.CompilerParams(
            collective_id=0, has_side_effects=True, vmem_limit_bytes=56 * 1024 * 1024
        ),
    )
    rate_wide = jnp.repeat(rate_weight[0], SLOT, axis=1)
    bias_wide = jnp.repeat(rate_bias, SLOT, axis=1)
    decay_wide = jnp.repeat(decay_rate, SLOT, axis=1)

    def layer(stream):
        return tick(
            stream,
            norm_gain,
            value_weight[0],
            shared_weight[0],
            rate_wide,
            bias_wide,
            decay_wide,
            lw,
            out_gain,
            out_weight[0],
        )

    handed = layer(activations[0])
    return layer(passed_along(handed, "section", 1))[None]


def solution(mesh):
    placed = (
        P("section", "seq", None),
        P("section", None),
        P("section", None, None),
        P("section", None, None),
        P("section", None, None),
        P("section", None),
        P("section", None),
        P("section", None, None, None),
        P("section", "seq", None),
        P("section", None),
        P("section", None, None),
    )
    return jax.shard_map(
        body, mesh=mesh, in_specs=placed, out_specs=P("section", "seq", None), check_vma=False
    )
```

profile of v0, /device:TPU:0, one launch (start us, length us, event | category | flops | bytes accessed | tf_op | source)
XLA Modules:
  0.0 136.1 jit_solution(10759162557655067648)
XLA Ops:
  0.0 0.7 broadcast_in_dim.40
  0.7 0.6 broadcast_in_dim.41.bias_ref
  1.4 0.7 broadcast_in_dim.42
  2.1 0.6 broadcast_in_dim.43.rate_ref
  2.7 0.9 copy.19
  3.6 0.9 copy.15
  4.5 0.8 broadcast_in_dim.39
  5.3 1.0 copy.17.wr_ref
  6.4 0.3 broadcast_select_fusion
  6.7 0.9 select_n.9.table_ref
  7.6 0.7 pad.8.ids_ref
  8.3 2.2 %shard_map.115.lw_ref = f32[512,128]{1,0:T(8,128)} custom-call(bf16[512,128]{1,0:T(8,128)(2,1)} %pad.8.ids_ref, f32[256,128]{1,0:T(8,128)} %select_n.9.table_ref), custom_call_target="tpu_custom_call" | custom-call | tf_op jit(solution)/shard_map/pallas_call | solution.py:306
  10.5 49.9 %shard_map.116 = bf16[512,2048]{1,0:T(8,128)(2,1)} custom-call(bf16[512,2048]{1,0:T(8,128)(2,1)} %bitcast.24, f32[1,2048]{1,0:T(1,128)} %gain_ref.3, bf16[2048,1024]{1,0:T(8,128)(2,1)} %bitcast.16, bf16[2048,256]{1,0:T(8,128)(2,1)} %bitcast.21, bf16[2048,128]{1,0:T(8,128)(2,1)} %copy.17.wr_ref, f32[1,128]{1,0:T(1,128)} %broadcast_in_dim.41.bias_ref, ...), custom_call_target="tpu_custom_call" | custom-call | tf_op jit(solution)/shard_map/pallas_call | solution.py:342
  60.4 0.2 collective-permute-start
  60.7 25.7 %collective-permute-done.x_ref = bf16[512,2048]{1,0:T(8,128)(2,1)S(1)} collective-permute-done((bf16[512,2048]{1,0:T(8,128)(2,1)}, bf16[512,2048]{1,0:T(8,128)(2,1)S(1)}, u32[]{:S(2)}, u32[]{:S(2)}) %collective-permute-start) | collective-permute-done | bytes 2097184 | tf_op jit(solution)/shard_map/ppermute | solution.py:272
  86.3 0.0 copy-start
  86.3 1.3 copy-done
  87.7 45.3 %shard_map.117 = bf16[512,2048]{1,0:T(8,128)(2,1)} custom-call(bf16[512,2048]{1,0:T(8,128)(2,1)} %copy-done, f32[1,2048]{1,0:T(1,128)} %gain_ref.3, bf16[2048,1024]{1,0:T(8,128)(2,1)} %bitcast.17, bf16[2048,256]{1,0:T(8,128)(2,1)} %bitcast.22, bf16[2048,128]{1,0:T(8,128)(2,1)} %copy.17.wr_ref, f32[1,128]{1,0:T(1,128)} %broadcast_in_dim.41.bias_ref, ...), custom_call_target="tpu_custom_call" | custom-call | tf_op jit(solution)/shard_map/pallas_call | solution.py:342
  133.0 3.2 %copy.21 = bf16[1,512,2048]{2,1,0:T(8,128)(2,1)} copy(bf16[1,512,2048]{2,1,0:T(8,128)(2,1)} %bitcast.20) | data formatting | bytes 4194304
  (3 shorter events, 0.0 us)
Async XLA Ops:
  60.4 25.9 %collective-permute-start = (bf16[512,2048]{1,0:T(8,128)(2,1)}, bf16[512,2048]{1,0:T(8,128)(2,1)S(1)}, u32[]{:S(2)}, u32[]{:S(2)}) collective-permute-start(bf16[512,2048]{1,0:T(8,128)(2,1)} %shard_map.116), channel_id=1, source_target_pairs={{24,0},{0,8},{8,16},{16,24},{25,1},{1,9},{9,17},{17,25},{26,2},{2,... | collective-permute-start | bytes 6291464 | tf_op jit(solution)/shard_map/ppermute | solution.py:272
  86.3 1.3 copy-start
where the time goes:
time: 136 us
  Pallas kernels  97.4 us (72%)
  waiting for transfers between devices  25.7 us (19%)
  local copies, waits for them, and re-layouts  12.4 us (9%)
    pallas_call x2, Pallas kernels, layer(): tick(stream, norm_gain, value_weight[0], shared_weight[0], rate_wide, bia...  95.2 us
    ppermute x1, waiting for transfers between devices, passed_along(): return lax.ppermute(block, axis, route)  25.7 us
    unnamed x5, local copies, waits for them, and re-layouts  6.25 us
  transfers between devices with their start and end apart: 1, of which 1 were waited for; matrix products, arithmetic and copies ran while one was open for 0% of the time, Pallas kernels for 0%

commit v1 on v0

v1 whole, which is shorter than its diff:
```python
import functools

import jax
import jax.numpy as jnp
from jax import lax
from jax.experimental import pallas as pl
from jax.experimental.pallas import tpu as pltpu
from jax.sharding import PartitionSpec as P

EPSILON = 1e-05
CHUNK = 128
SLOT = 16
F32 = jnp.float32
BF16 = jnp.bfloat16


def dot(a, b):
    return jnp.dot(a, b, preferred_element_type=F32)


def dot_nt(a, b):
    return lax.dot_general(a, b, (((1,), (1,)), ((), ())), preferred_element_type=F32)


def dot_tn(a, b):
    return lax.dot_general(a, b, (((0,), (0,)), ((), ())), preferred_element_type=F32)


def iota(shape, dim):
    return lax.broadcasted_iota(jnp.int32, shape, dim)


def split3(x):
    hi = x.astype(BF16)
    rest = x - hi.astype(F32)
    mid = rest.astype(BF16)
    return hi, mid, (rest - mid.astype(F32)).astype(BF16)


def spread(row, heads, width):
    rows = row.shape[0]
    return jnp.concatenate(
        [
            jnp.broadcast_to(row[:, h * SLOT : h * SLOT + 1], (rows, width))
            for h in range(heads)
        ],
        axis=1,
    )


def widen(v, heads):
    expand = (iota((heads, heads * SLOT), 0) == iota((heads, heads * SLOT), 1) // SLOT).astype(BF16)
    return sum(dot(part, expand) for part in split3(v))


def ticks_kernel(
    heads,
    bits,
    tok_bits,
    pieces,
    x_ref,
    gain_ref,
    wv_hbm,
    ws_hbm,
    wr_ref,
    bias_ref,
    rate_ref,
    table_ref,
    ids_ref,
    out_gain_ref,
    wo_hbm,
    nmix,
    arrived_hbm,
    wv_ref,
    ws_ref,
    wo_ref,
    lw_ref,
    normed,
    step,
    local,
    vals,
    qk,
    acc,
    parts,
    inner,
    subtree,
    totals_ref,
    handed,
    arrived,
    send,
    recv,
    load_sem,
    send_sem,
    recv_sem,
    hand_send_sem,
    hand_recv_sem,
):
    rows, width = x_ref.shape
    inner_width = heads * CHUNK
    n = CHUNK
    chunks = rows // CHUNK
    inner_bits = chunks.bit_length() - 1
    base = tok_bits - inner_bits
    pair = inner_width // pieces
    pair_heads = heads // pieces
    me = lax.axis_index("seq")
    sections = lax.axis_size("section")
    section = lax.axis_index("section")
    following = (section + 1) % sections
    previous = (section + sections - 1) % sections
    mesh_ids = pl.DeviceIdType.MESH

    def bit_of(d):
        return (me // (1 << d)) % 2

    def partner_of(d):
        return me + (1 << d) * (1 - 2 * bit_of(d))

    loads = [
        pltpu.make_async_copy(src, dst, load_sem.at[i])
        for i, (src, dst) in enumerate(((ws_hbm, ws_ref), (wv_hbm, wv_ref), (wo_hbm, wo_ref)))
    ]
    for load in loads:
        load.start()
    barrier = pltpu.get_barrier_semaphore()
    for d in range(bits):
        pl.semaphore_signal(barrier, inc=1, device_id={"seq": partner_of(d)}, device_id_type=mesh_ids)
    for other in (following, previous):
        pl.semaphore_signal(barrier, inc=1, device_id={"section": other}, device_id_type=mesh_ids)
    pl.semaphore_wait(barrier, bits + 2)

    lanes = table_ref.shape[0]
    spot = (lanes, heads * SLOT)
    table = jnp.where(
        iota(spot, 0) // SLOT == iota(spot, 1) % SLOT, widen(table_ref[...], heads), 0.0
    )
    pick = iota((CHUNK, lanes), 0) == iota((CHUNK, lanes), 1) // SLOT
    ids = dot(ids_ref[...], pick.astype(BF16))
    onehot = (ids == (iota(ids.shape, 1) % SLOT).astype(F32)).astype(BF16)
    lw_ref[...] = sum(dot(onehot, part) for part in split3(table))
    rate_wide = dot(wr_ref[...], (iota((heads, heads * SLOT), 0) == iota((heads, heads * SLOT), 1) // SLOT).astype(BF16)).astype(BF16)
    bias = widen(jnp.broadcast_to(bias_ref[...], (8, heads)), heads)[:1, :]
    rate = widen(jnp.broadcast_to(rate_ref[...], (8, heads)), heads)[:1, :]
    tri = (iota((CHUNK, CHUNK), 0) >= iota((CHUNK, CHUNK), 1)).astype(BF16)

    position_t = iota((CHUNK, CHUNK), 0)
    position_u = iota((CHUNK, CHUNK), 1)
    causal = position_t >= position_u
    flipped = position_t ^ position_u
    level = jnp.zeros((CHUNK, CHUNK), jnp.int32)
    for b in range(base):
        level = level + (flipped >= (1 << b)).astype(jnp.int32)

    def handoff(c):
        at = pl.ds(pl.multiple_of(c * CHUNK, CHUNK), CHUNK)
        return pltpu.make_async_remote_copy(
            src_ref=handed.at[at, :],
            dst_ref=arrived.at[at, :],
            send_sem=hand_send_sem.at[c],
            recv_sem=hand_recv_sem.at[c],
            device_id={"section": following},
            device_id_type=mesh_ids,
        )

    def exchange(t, d, p):
        return pltpu.make_async_remote_copy(
            src_ref=send.at[t, d, p],
            dst_ref=recv.at[t, d, p],
            send_sem=send_sem.at[t, d, p],
            recv_sem=recv_sem.at[t, d, p],
            device_id={"seq": partner_of(d)},
            device_id_type=mesh_ids,
        )

    def project(first, size, source, t):
        group = pl.ds(pl.multiple_of(first * CHUNK, CHUNK), size)

        @pl.loop(0, size // CHUNK)
        def _(i):
            at = pl.ds(pl.multiple_of((first + i) * CHUNK, CHUNK), CHUNK)
            x = source[at, :].astype(F32)
            scale = lax.rsqrt(jnp.mean(x * x, axis=-1, keepdims=True) + EPSILON)
            normed[at, :] = (x * scale * gain_ref[...]).astype(BF16)

        u = dot(normed[group, :], rate_wide) + bias
        step[group, :] = jnp.maximum(u, 0.0) + jnp.log1p(jnp.exp(-jnp.abs(u)))
        if t == 0:
            loads[0].wait()
        qk[group, :] = dot(normed[group, :], ws_ref[...]).astype(BF16)
        if t == 0:
            loads[1].wait()
        for p in range(pieces):
            raw = dot(normed[group, :], wv_ref[:, p * pair : (p + 1) * pair])
            for i in range(pair_heads):
                h = p * pair_heads + i
                vals[group, h * CHUNK : (h + 1) * CHUNK] = (
                    raw[:, i * CHUNK : (i + 1) * CHUNK] * step[group, h * SLOT : h * SLOT + 1]
                ).astype(BF16)

        @pl.loop(0, size // CHUNK)
        def _(i):
            c = first + i
            at = pl.ds(pl.multiple_of(c * CHUNK, CHUNK), CHUNK)
            cs = sum(dot(tri, part) for part in split3(-rate * step[at, :]))
            local[at, :] = cs
            whole = cs[CHUNK - 1 :, :]
            totals_ref[c] = jnp.broadcast_to(whole, (8, heads * SLOT))
            fade = jnp.exp(whole - cs)
            decayed = (vals[at, :].astype(F32) * spread(fade, heads, CHUNK)).astype(BF16)
            parts[at, :] = dot_tn(qk[at, :n], decayed)

    def tick(t):
        if t == 0:
            project(0, rows, x_ref, t)
        else:

            @pl.loop(0, chunks)
            def _(c):
                handoff(c).wait_recv()
                project(c, CHUNK, arrived, t)

        totals = [totals_ref[c][:1, :] for c in range(chunks)]
        group_totals = {}
        for e in range(inner_bits + 1):
            for g in range(chunks >> e):
                group_totals[e, g] = sum(totals[(g << e) + 1 : (g + 1) << e], totals[g << e])
        slots = [(e, g) for e in range(inner_bits) for g in range(1, chunks >> e, 2)]
        wide = {
            key: spread(value, heads, CHUNK)
            for key, value in group_totals.items()
        }

        def put(d, p, decay):
            cols = slice(p * pair, (p + 1) * pair)
            send[t, d, p, :n, :] = subtree[:, cols].astype(BF16)
            row = iota((SLOT, pair), 0)
            tail = jnp.zeros((SLOT, pair), F32)
            for i, part in enumerate(split3(decay)):
                tail = jnp.where(row == i, part.astype(F32), tail)
            send[t, d, p, n:, :] = tail.astype(BF16)
            exchange(t, d, p).start()

        decay = wide[inner_bits, 0]
        for p in range(pieces):
            cols = slice(p * pair, (p + 1) * pair)
            group = [parts[c * CHUNK : (c + 1) * CHUNK, cols] for c in range(chunks)]
            slot = 0
            for e in range(inner_bits):
                merged = []
                for g in range(0, len(group), 2):
                    inner[slot * n : (slot + 1) * n, cols] = group[g].astype(BF16)
                    slot += 1
                    merged.append(
                        group[g] * jnp.exp(wide[e, g + 1][:, cols]) + group[g + 1]
                    )
                group = merged
            subtree[:, cols] = group[0]
            put(0, p, decay[:, cols])

        def near(c):
            at = slice(c * CHUNK, (c + 1) * CHUNK)
            scores = jnp.where(causal, dot_nt(qk[at, n:], qk[at, :n]), 0.0)
            run = local[at, :]
            run_t = run.T
            weights = lw_ref[at, :]
            for h in range(heads):
                lane = h * SLOT
                exponent = run[:, lane : lane + 1] - run_t[lane : lane + 1, :]
                weight = jnp.take_along_axis(weights, level + lane, axis=1)
                mixing = (weight * jnp.exp(jnp.minimum(exponent, 0.0)) * scores).astype(BF16)
                col = slice(h * CHUNK, (h + 1) * CHUNK)
                acc[at, col] = dot(mixing, vals[at, col])

        def add_level(at, coef, l, state):
            far = dot(qk[at, n:], state)
            for h in range(heads):
                col = slice(h * CHUNK, (h + 1) * CHUNK)
                acc[at, col] += coef[:, h * SLOT + l : h * SLOT + l + 1] * far[:, col]

        def near_states(c):
            at = slice(c * CHUNK, (c + 1) * CHUNK)
            for slot, (e, g) in enumerate(slots):
                if c >> e != g:
                    continue
                prefix = sum(totals[g << e : c], jnp.zeros_like(totals[0]))
                coef = lw_ref[at, :] * jnp.exp(local[at, :] + prefix)
                add_level(at, coef, base + e + 1, inner[slot * n : (slot + 1) * n, :])

        def far_state(d, prefix):
            factor = jnp.where(bit_of(d) == 1, jnp.exp(prefix), 0.0)
            return jnp.concatenate(
                [
                    (recv[t, d, p, :n, :].astype(F32) * factor[:, p * pair : (p + 1) * pair]).astype(BF16)
                    for p in range(pieces)
                ],
                axis=1,
            )

        def distant(c, d, state):
            at = slice(c * CHUNK, (c + 1) * CHUNK)
            before = sum(totals[:c], jnp.zeros_like(totals[0]))
            coef = lw_ref[at, :] * jnp.exp(local[at, :] + before)
            add_level(at, coef, tok_bits + 1 + d, state)

        work = [functools.partial(near, c) for c in range(chunks)]
        work += [functools.partial(near_states, c) for c in range(1, chunks)]
        prefix = jnp.zeros_like(decay)
        prefixes = []
        taken = 0
        for d in range(bits):
            stop = len(work) * (2 * d + 2) // (2 * bits) if d < bits - 1 else len(work)
            for item in work[taken:stop]:
                item()
            taken = stop
            if d >= 2:
                for e in range(d - 2, d) if d == bits - 1 else (d - 2,):
                    state = far_state(e, prefixes[e])
                    for c in range(chunks):
                        distant(c, e, state)
            upper = bit_of(d) == 1
            prefixes.append(prefix)
            found = []
            for p in range(pieces):
                cols = slice(p * pair, (p + 1) * pair)
                exchange(t, d, p).wait()
                if d == bits - 1:
                    continue
                tail = recv[t, d, p, n:, :].astype(F32)
                there = tail[0:1, :] + tail[1:2, :] + tail[2:3, :]
                here = decay[:, cols]
                mine = jnp.exp(jnp.where(upper, 0.0, there))
                theirs = jnp.exp(jnp.where(upper, here, 0.0))
                subtree[:, cols] = subtree[:, cols] * mine + recv[t, d, p, :n, :].astype(F32) * theirs
                found.append(there)
                put(d + 1, p, here + there)
            if d < bits - 1:
                there = jnp.concatenate(found, axis=1)
                prefix = jnp.where(upper, prefix + there, prefix)
                decay = decay + there
        rest = range(bits - 1, bits) if bits >= 3 else range(bits)
        states = [(d, far_state(d, prefixes[d])) for d in rest]
        if t == 0:
            loads[2].wait()
        for c in range(chunks):
            at = slice(c * CHUNK, (c + 1) * CHUNK)
            for d, state in states:
                distant(c, d, state)
            mixed = acc[at, :]
            scale = lax.rsqrt(jnp.mean(mixed * mixed, axis=-1, keepdims=True) + EPSILON)
            nmix[at, :] = (mixed * scale * out_gain_ref[...]).astype(BF16)
            if t == 0:

                @pl.loop(0, width // (2 * CHUNK))
                def _(i):
                    col = pl.ds(pl.multiple_of(i * 2 * CHUNK, 2 * CHUNK), 2 * CHUNK)
                    handed[at, col] = (
                        x_ref[at, col].astype(F32) + dot(nmix[at, :], wo_ref[:, col])
                    ).astype(BF16)

                handoff(c).start()

    tick(0)
    tick(1)
    keep = pltpu.make_async_copy(arrived, arrived_hbm, load_sem.at[0])
    keep.start()
    for c in range(chunks):
        handoff(c).wait_send()
    keep.wait()


def body(
    activations,
    norm_gain,
    value_weight,
    shared_weight,
    rate_weight,
    rate_bias,
    decay_rate,
    level_table,
    level_ids,
    out_gain,
    out_weight,
):
    rows, width = activations.shape[1:]
    heads = rate_bias.shape[1]
    buckets, levels = level_table.shape[1:3]
    inner_width = value_weight.shape[2]
    tok_bits = rows.bit_length() - 1
    bits = lax.axis_size("seq").bit_length() - 1
    chunks = rows // CHUNK
    pieces = heads // 2
    table = jnp.transpose(level_table[0], (1, 0, 2))
    table = jnp.pad(table, ((0, SLOT - levels), (0, SLOT - buckets), (0, 0)))
    table = table.reshape(SLOT * SLOT, heads)
    ids = jnp.pad(level_ids[0].astype(BF16), ((0, 0), (0, CHUNK - levels)))
    hbm = pl.BlockSpec(memory_space=pl.ANY)
    near = pl.BlockSpec(memory_space=pltpu.VMEM)
    states = (2, bits, pieces, CHUNK + SLOT, inner_width // pieces)
    normed_mix, arrived = pl.pallas_call(
        functools.partial(ticks_kernel, heads, bits, tok_bits, pieces),
        out_shape=(
            jax.ShapeDtypeStruct((rows, inner_width), BF16),
            jax.ShapeDtypeStruct((rows, width), BF16),
        ),
        in_specs=[near, near, hbm, hbm, near, near, near, near, near, near, hbm],
        out_specs=(near, hbm),
        scratch_shapes=[
            pltpu.VMEM(value_weight.shape[1:], BF16),
            pltpu.VMEM(shared_weight.shape[1:], BF16),
            pltpu.VMEM(out_weight.shape[1:], BF16),
            pltpu.VMEM((rows, heads * SLOT), F32),
            pltpu.VMEM((rows, width), BF16),
            pltpu.VMEM((rows, heads * SLOT), F32),
            pltpu.VMEM((rows, heads * SLOT), F32),
            pltpu.VMEM((rows, inner_width), BF16),
            pltpu.VMEM((rows, shared_weight.shape[2]), BF16),
            pltpu.VMEM((rows, inner_width), F32),
            pltpu.VMEM((rows, inner_width), F32),
            pltpu.VMEM((max(chunks - 1, 1) * CHUNK, inner_width), BF16),
            pltpu.VMEM((CHUNK, inner_width), F32),
            pltpu.VMEM((chunks, 8, heads * SLOT), F32),
            pltpu.VMEM((rows, width), BF16),
            pltpu.VMEM((rows, width), BF16),
            pltpu.VMEM(states, BF16),
            pltpu.VMEM(states, BF16),
            pltpu.SemaphoreType.DMA((3,)),
            pltpu.SemaphoreType.DMA(states[:3]),
            pltpu.SemaphoreType.DMA(states[:3]),
            pltpu.SemaphoreType.DMA((chunks,)),
            pltpu.SemaphoreType.DMA((chunks,)),
        ],
        compiler_params=pltpu.CompilerParams(
            collective_id=0, has_side_effects=True, vmem_limit_bytes=56 * 1024 * 1024
        ),
    )(
        activations[0],
        norm_gain,
        value_weight[0],
        shared_weight[0],
        rate_weight[0],
        rate_bias,
        decay_rate,
        table,
        ids,
        out_gain,
        out_weight[0],
    )
    return (arrived.astype(F32) + dot(normed_mix, out_weight[0])).astype(BF16)[None]


def solution(mesh):
    placed = (
        P("section", "seq", None),
        P("section", None),
        P("section", None, None),
        P("section", None, None),
        P("section", None, None),
        P("section", None),
        P("section", None),
        P("section", None, None, None),
        P("section", "seq", None),
        P("section", None),
        P("section", None, None),
    )
    return jax.shard_map(
        body, mesh=mesh, in_specs=placed, out_specs=P("section", "seq", None), check_vma=False
    )
```

time: 136 us -> 96.6 us (0.71)
  waiting for transfers between devices: 25.7 us -> 0 us
  Pallas kernels: 97.4 us -> 85.7 us
  local copies, waits for them, and re-layouts: 12.4 us -> 4.87 us
  matrix products: 0 us -> 5.58 us
    ppermute x1 -> x0, waiting for transfers between devices: 25.7 us -> none  [passed_along(): return lax.ppermute(block, axis, route)]
    pallas_call x3 -> x1, Pallas kernels: 97.4 us -> 85.7 us  [body(): pl.pallas_call(functools.partial(ticks_kernel, heads, bits, tok_bits, pie...]
    dot_general x0 -> x1, matrix products: none -> 5.58 us  [dot(): return jnp.dot(a, b, preferred_element_type=F32)]
    broadcast_in_dim x5 -> x0, local copies, waits for them, and re-layouts: 3.52 us -> none  [the longest x2 1.37 us: body(): bias_wide = jnp.repeat(rate_bias, SLOT, axis=1)]
    unnamed x5, local copies, waits for them, and re-layouts: 6.25 us -> 3.53 us
  transfers between devices with their start and end apart: 1 -> 0, of which waited for: 1 -> 0; matrix products, arithmetic and copies ran while one was open for 0% -> 0% of each run, Pallas kernels for 0% -> 0%
where the time goes in v1:
time: 96.6 us; the launch traced here: 96.3 us
  Pallas kernels  85.7 us (89%)
  matrix products  5.58 us (6%)
  local copies, waits for them, and re-layouts  4.87 us (5%)
    pallas_call x1, Pallas kernels, body(): pl.pallas_call(functools.partial(ticks_kernel, heads, bits, tok_bits, pie...  85.7 us
    dot_general x1, matrix products, dot(): return jnp.dot(a, b, preferred_element_type=F32)  5.58 us
    unnamed x5, local copies, waits for them, and re-layouts  3.53 us

profile of v1, /device:TPU:0, one launch (start us, length us, event | category | flops | bytes accessed | tf_op | source)
XLA Modules:
  0.0 96.3 jit_solution(8920812225165441143)
XLA Ops:
  0.0 0.9 copy.15
  0.9 0.7 pad.8.clone
  1.6 0.9 copy.14
  2.5 0.7 pad.9.ids_ref
  3.1 1.8 %copy.12 = bf16[1,2048,8]{2,1,0:T(8,128)(2,1)} copy(bf16[1,2048,8]{1,2,0:T(8,128)(2,1)} %param.15) | data formatting | bytes 65536 | tf_op args[4]
  4.9 0.0 copy-start
  4.9 85.7 %shard_map.109 = (bf16[512,1024]{1,0:T(8,128)(2,1)}, bf16[512,2048]{1,0:T(8,128)(2,1)}) custom-call(bf16[512,2048]{1,0:T(8,128)(2,1)} %bitcast.18, f32[1,2048]{1,0:T(1,128)} %gain_ref.1, bf16[2048,1024]{1,0:T(8,128)(2,1)} %bitcast.16, bf16[2048,256]{1,0:T(8,128)(2,1)} %bitcast.20, bf16[2048,8]{1,0:T(8,128)(2,1)} %bitcast.19, f32[1,8]{1,0:T(1,128)} %bias_ref.1, ...), custom_call_target="tpu_custom_call" | custom-call | tf_op jit(solution)/shard_map/pallas_call | solution.py:399
  90.7 0.0 copy-done
  90.7 5.6 %fusion = bf16[1,512,2048]{2,1,0:T(8,128)(2,1)} fusion(bf16[512,1024]{1,0:T(8,128)(2,1)} %get-tuple-element.8, bf16[512,2048]{1,0:T(8,128)(2,1)} %get-tuple-element.7, bf16[1,1024,2048]{2,1,0:T(8,128)(2,1)S(1)} %copy-done), kind=kOutput, calls=%fused_computation.1 | convolution fusion | flops 2150629376 | bytes 9437184 | tf_op jit(solution)/shard_map/dot_general | solution.py:18
  (1 shorter events, 0.0 us)
Async XLA Ops:
  4.9 85.8 %copy-start = (bf16[1,1024,2048]{2,1,0:T(8,128)(2,1)S(1)}, bf16[1,1024,2048]{2,1,0:T(8,128)(2,1)}, u32[]{:S(2)}) copy-start(bf16[1,1024,2048]{2,1,0:T(8,128)(2,1)} %param.21) | copy-start | bytes 12582916

commit v2 on v1

--- a/solution.py
+++ b/solution.py
@@ -134,11 +134,13 @@
     table = jnp.where(
         iota(spot, 0) // SLOT == iota(spot, 1) % SLOT, widen(table_ref[...], heads), 0.0
     )
-    pick = iota((CHUNK, lanes), 0) == iota((CHUNK, lanes), 1) // SLOT
-    ids = dot(ids_ref[...], pick.astype(BF16))
+    levels = ids_ref.shape[0]
+    pick = iota((levels, lanes), 0) == iota((levels, lanes), 1) // SLOT
+    ids = dot_tn(ids_ref[...].astype(F32).astype(BF16), pick.astype(BF16))
     onehot = (ids == (iota(ids.shape, 1) % SLOT).astype(F32)).astype(BF16)
     lw_ref[...] = sum(dot(onehot, part) for part in split3(table))
-    rate_wide = dot(wr_ref[...], (iota((heads, heads * SLOT), 0) == iota((heads, heads * SLOT), 1) // SLOT).astype(BF16)).astype(BF16)
+    expand = iota((heads, heads * SLOT), 0) == iota((heads, heads * SLOT), 1) // SLOT
+    rate_wide = dot_tn(expand.astype(BF16), wr_ref[...]).astype(BF16)
     bias = widen(jnp.broadcast_to(bias_ref[...], (8, heads)), heads)[:1, :]
     rate = widen(jnp.broadcast_to(rate_ref[...], (8, heads)), heads)[:1, :]
     tri = (iota((CHUNK, CHUNK), 0) >= iota((CHUNK, CHUNK), 1)).astype(BF16)
@@ -182,7 +184,7 @@
             scale = lax.rsqrt(jnp.mean(x * x, axis=-1, keepdims=True) + EPSILON)
             normed[at, :] = (x * scale * gain_ref[...]).astype(BF16)
 
-        u = dot(normed[group, :], rate_wide) + bias
+        u = dot_nt(normed[group, :], rate_wide) + bias
         step[group, :] = jnp.maximum(u, 0.0) + jnp.log1p(jnp.exp(-jnp.abs(u)))
         if t == 0:
             loads[0].wait()
@@ -239,6 +241,26 @@
                 tail = jnp.where(row == i, part.astype(F32), tail)
             send[t, d, p, n:, :] = tail.astype(BF16)
             exchange(t, d, p).start()
+
+        def near(c):
+            at = slice(c * CHUNK, (c + 1) * CHUNK)
+            scores = jnp.where(causal, dot_nt(qk[at, n:], qk[at, :n]), 0.0)
+            run = local[at, :]
+            run_t = run.T
+            weights = lw_ref[at, :]
+            for h in range(heads):
+                lane = h * SLOT
+                exponent = run[:, lane : lane + 1] - run_t[lane : lane + 1, :]
+                weight = jnp.take_along_axis(weights, level + lane, axis=1)
+                mixing = (weight * jnp.exp(jnp.minimum(exponent, 0.0)) * scores).astype(BF16)
+                col = slice(h * CHUNK, (h + 1) * CHUNK)
+                acc[at, col] = dot(mixing, vals[at, col])
+
+        if t == 0:
+            @pl.when(section % 2 == 0)
+            def _():
+                for c in range(chunks):
+                    near(c)
 
         decay = wide[inner_bits, 0]
         for p in range(pieces):
@@ -257,20 +279,6 @@
             subtree[:, cols] = group[0]
             put(0, p, decay[:, cols])
 
-        def near(c):
-            at = slice(c * CHUNK, (c + 1) * CHUNK)
-            scores = jnp.where(causal, dot_nt(qk[at, n:], qk[at, :n]), 0.0)
-            run = local[at, :]
-            run_t = run.T
-            weights = lw_ref[at, :]
-            for h in range(heads):
-                lane = h * SLOT
-                exponent = run[:, lane : lane + 1] - run_t[lane : lane + 1, :]
-                weight = jnp.take_along_axis(weights, level + lane, axis=1)
-                mixing = (weight * jnp.exp(jnp.minimum(exponent, 0.0)) * scores).astype(BF16)
-                col = slice(h * CHUNK, (h + 1) * CHUNK)
-                acc[at, col] = dot(mixing, vals[at, col])
-
         def add_level(at, coef, l, state):
             far = dot(qk[at, n:], state)
             for h in range(heads):
@@ -302,7 +310,10 @@
             coef = lw_ref[at, :] * jnp.exp(local[at, :] + before)
             add_level(at, coef, tok_bits + 1 + d, state)
 
-        work = [functools.partial(near, c) for c in range(chunks)]
+        def near_late(c):
+            pl.when(section % 2 == 1)(functools.partial(near, c))
+
+        work = [functools.partial(near_late if t == 0 else near, c) for c in range(chunks)]
         work += [functools.partial(near_states, c) for c in range(1, chunks)]
         prefix = jnp.zeros_like(decay)
         prefixes = []
@@ -368,6 +379,10 @@
     keep.wait()
 
 
+def out_kernel(mix_ref, x_ref, wo_ref, y_ref):
+    y_ref[...] = (x_ref[...].astype(F32) + dot(mix_ref[...], wo_ref[...])).astype(BF16)
+
+
 def body(
     activations,
     norm_gain,
@@ -392,7 +407,7 @@
     table = jnp.transpose(level_table[0], (1, 0, 2))
     table = jnp.pad(table, ((0, SLOT - levels), (0, SLOT - buckets), (0, 0)))
     table = table.reshape(SLOT * SLOT, heads)
-    ids = jnp.pad(level_ids[0].astype(BF16), ((0, 0), (0, CHUNK - levels)))
+    ids = level_ids[0].T
     hbm = pl.BlockSpec(memory_space=pl.ANY)
     near = pl.BlockSpec(memory_space=pltpu.VMEM)
     states = (2, bits, pieces, CHUNK + SLOT, inner_width // pieces)
@@ -437,7 +452,7 @@
         norm_gain,
         value_weight[0],
         shared_weight[0],
-        rate_weight[0],
+        rate_weight[0].T,
         rate_bias,
         decay_rate,
         table,
@@ -445,7 +460,19 @@
         out_gain,
         out_weight[0],
     )
-    return (arrived.astype(F32) + dot(normed_mix, out_weight[0])).astype(BF16)[None]
+    tile = 2 * CHUNK
+    column = pl.BlockSpec((rows, tile), lambda i: (0, i))
+    return pl.pallas_call(
+        out_kernel,
+        grid=(width // tile,),
+        out_shape=jax.ShapeDtypeStruct((rows, width), BF16),
+        in_specs=[
+            pl.BlockSpec((rows, inner_width), lambda i: (0, 0)),
+            column,
+            pl.BlockSpec((inner_width, tile), lambda i: (0, i)),
+        ],
+        out_specs=column,
+    )(normed_mix, arrived, out_weight[0])[None]
 
 
 def solution(mesh):

time: 96.6 us -> 93.3 us (0.966)
  matrix products: 5.58 us -> 0 us
  Pallas kernels: 85.7 us -> 89.9 us
  local copies, waits for them, and re-layouts: 4.87 us -> 2.91 us
    pallas_call x0 -> x1, Pallas kernels: none -> 8.44 us  [body(): pl.pallas_call(out_kernel, grid=(width // tile,), out_shape=jax.ShapeDtyp...]
    dot_general x1 -> x0, matrix products: 5.58 us -> none  [dot(): return jnp.dot(a, b, preferred_element_type=F32)]
    pallas_call x1, Pallas kernels: 85.7 us -> 81.5 us  [body(): pl.pallas_call(functools.partial(ticks_kernel, heads, bits, tok_bits, pie...]
    unnamed x5 -> x2, local copies, waits for them, and re-layouts: 3.53 us -> 2.24 us
where the time goes in v2:
time: 93.3 us; the launch traced here: 92.8 us
  Pallas kernels  89.9 us (96%)
  local copies, waits for them, and re-layouts  2.91 us (3%)
    pallas_call x1, Pallas kernels, body(): pl.pallas_call(functools.partial(ticks_kernel, heads, bits, tok_bits, pie...  81.5 us
    pallas_call x1, Pallas kernels, body(): pl.pallas_call(out_kernel, grid=(width // tile,), out_shape=jax.ShapeDtyp...  8.44 us
    unnamed x2, local copies, waits for them, and re-layouts  2.24 us

profile of v2, /device:TPU:0, one launch (start us, length us, event | category | flops | bytes accessed | tf_op | source)
XLA Modules:
  0.0 92.8 jit_solution(9041714225062196533)
XLA Ops:
  0.0 1.3 %copy.16 = s32[1,512,13]{1,2,0:T(8,128)} copy(s32[1,512,13]{1,0,2:T(1,128)} %param.19) | data formatting | bytes 53248
  1.4 0.9 copy.14
  2.2 0.7 pad.4.clone
  2.9 81.5 %shard_map.109 = (bf16[512,1024]{1,0:T(8,128)(2,1)}, bf16[512,2048]{1,0:T(8,128)(2,1)}) custom-call(bf16[512,2048]{1,0:T(8,128)(2,1)} %bitcast.20, f32[1,2048]{1,0:T(1,128)} %gain_ref.1, bf16[2048,1024]{1,0:T(8,128)(2,1)} %bitcast.19, bf16[2048,256]{1,0:T(8,128)(2,1)} %bitcast.21, bf16[8,2048]{1,0:T(8,128)(2,1)} %bitcast.25, f32[1,8]{1,0:T(1,128)} %bias_ref.1, ...), custom_call_target="tpu_custom_call" | custom-call | tf_op jit(solution)/shard_map/pallas_call | solution.py:414
  84.4 8.4 %shard_map.110 = bf16[512,2048]{1,0:T(8,128)(2,1)} custom-call(bf16[512,1024]{1,0:T(8,128)(2,1)} %get-tuple-element.7.mix_ref, bf16[512,2048]{1,0:T(8,128)(2,1)} %get-tuple-element.8.x_ref, bf16[1024,2048]{1,0:T(8,128)(2,1)} %bitcast.18), custom_call_target="tpu_custom_call" | custom-call | tf_op jit(solution)/shard_map/pallas_call | solution.py:465
